TPU v7x, 128 devices: a whole 4x4x4 slice. The times are simulated.
128 devices in a mesh: dp: 8 (over x, y_lo), seq: 16 (over z, y_hi, core).
Axes of the slice: x: 4, y: 4 (y_hi: 2, y_lo: 2; y = y_hi * 2 + y_lo), z: 4, core: 2. Of those that a mesh axis runs over, the one named last changes fastest.
Arguments:
- queries: bfloat16 [8, 3072, 4096], P('dp', 'seq'), may hold values from -9 to 9
- key_rows: bfloat16 [8, 3072, 4096], P('dp', 'seq'), may hold values from -9 to 9
- value_rows: bfloat16 [8, 3072, 4096], P('dp', 'seq'), may hold values from -12 to 12
- residual: bfloat16 [8, 3072, 5120], P('dp', 'seq'), may hold values from -6 to 6
- gate_scale: float32 [8, 5120], P('dp'), may hold values from 0.25 to 1.5
- out_weight: bfloat16 [4096, 5120], P('seq'), may hold values from -0.09375 to 0.09375
- adapter_down: bfloat16 [4096, 64], replicated, may hold values from -0.09375 to 0.09375
- adapter_up: bfloat16 [64, 5120], replicated, may hold values from -0.75 to 0.75
- cotangent: bfloat16 [8, 3072, 5120], P('dp', 'seq'), may hold values from -0.038085938 to 0.038085938
- clip_lengths: int32 [8], P('dp'), may hold values from 1536 to 3072, as said below
Outputs:
- block_out: bfloat16 [8, 3072, 5120], P('dp', 'seq')
- grad_down: float32 [4096, 64], replicated
- grad_up: float32 [64, 5120], replicated
Inputs may be any that keep to these rules, and one draw needn't show every extreme that they name: `clip_lengths`: some clip has all 3072 tokens valid.
All inputs are finite; a program needn't handle non-finite values.
Results may differ from a plain program's by a relative error of at most 0.012.
Values may be sent and summed in bfloat16 or wider, within the bound.
A program may use at most 192 MiB of HBM per device.

v0:
```python
import jax
import jax.numpy as jnp
from jax import lax
from jax.sharding import PartitionSpec as P

HEAD_DIM = 128


def attend_heads(query_part, key_part, value_part, length):
    total_rows = query_part.shape[0]
    head_count = query_part.shape[1]
    head_size = query_part.shape[2]
    block_rows = min(512, total_rows)
    factor = HEAD_DIM ** (-0.5)
    live_keys = jnp.arange(total_rows, dtype=jnp.int32) < length
    blocks = query_part.reshape(total_rows // block_rows, block_rows, head_count, head_size)

    def one_block(query_block):
        scores = (
            jnp.einsum("qhe,khe->hqk", query_block, key_part, preferred_element_type=jnp.float32)
            * factor
        )
        scores = jnp.where(live_keys[None, None, :], scores, -1e30)
        largest = jnp.max(scores, axis=2, keepdims=True)
        powers = jnp.exp(scores - largest)
        weights = (powers / jnp.sum(powers, axis=2, keepdims=True)).astype(jnp.bfloat16)
        return jnp.einsum(
            "hqk,khe->qhe", weights, value_part, preferred_element_type=jnp.float32
        ).astype(jnp.bfloat16)

    return lax.map(one_block, blocks).reshape(total_rows, head_count, head_size)


def to_tokens(head_mixed):
    swapped = lax.all_to_all(head_mixed, "seq", split_axis=0, concat_axis=1, tiled=True)
    return swapped.reshape(swapped.shape[0], swapped.shape[1] * swapped.shape[2])


def on_device(
    queries,
    key_rows,
    value_rows,
    residual,
    gate_scale,
    out_weight,
    adapter_down,
    adapter_up,
    cotangent,
    clip_lengths,
):
    tokens = queries.shape[1]
    full_width = queries.shape[2]
    length = clip_lengths[0]
    heads_all = full_width // HEAD_DIM
    groups = lax.axis_size("seq")
    group_heads = heads_all // groups

    def split_heads(matrix_in):
        return matrix_in[0].reshape(tokens, groups, group_heads, HEAD_DIM)

    mixed = attend_heads(
        lax.all_to_all(split_heads(queries), "seq", split_axis=1, concat_axis=0, tiled=True)[:, 0],
        lax.all_to_all(split_heads(key_rows), "seq", split_axis=1, concat_axis=0, tiled=True)[:, 0],
        lax.all_to_all(split_heads(value_rows), "seq", split_axis=1, concat_axis=0, tiled=True)[
            :, 0
        ],
        length,
    )
    exchanged = mixed[:, None]
    head_mixed = exchanged[:, 0]
    seq_len = head_mixed.shape[0]
    local_cols = head_mixed.shape[1] * head_mixed.shape[2]
    head_rows = head_mixed.reshape(seq_len, local_cols)
    gate_row = gate_scale[0][None, :]
    token_rows = None
    token_rows = to_tokens(head_mixed)
    low_rank = jnp.dot(token_rows, adapter_down, preferred_element_type=jnp.float32).astype(
        jnp.bfloat16
    )
    base = lax.psum_scatter(
        jnp.dot(head_rows, out_weight, preferred_element_type=jnp.float32).astype(jnp.bfloat16),
        "seq",
        scatter_dimension=0,
        tiled=True,
    ).astype(jnp.float32)
    delta = jnp.dot(low_rank, adapter_up, preferred_element_type=jnp.float32)
    block_out = (residual[0].astype(jnp.float32) + gate_row * (base + delta)).astype(jnp.bfloat16)[
        None
    ]
    scaled = (cotangent[0].astype(jnp.float32) * gate_row).astype(jnp.bfloat16)
    up_part = jnp.dot(low_rank.T, scaled, preferred_element_type=jnp.float32)
    low_grad = jnp.dot(scaled, adapter_up.T, preferred_element_type=jnp.float32).astype(
        jnp.bfloat16
    )
    down_part = jnp.dot(token_rows.T, low_grad, preferred_element_type=jnp.float32)
    grad_down, grad_up = lax.psum((down_part, up_part), ("dp", "seq"))
    return (block_out, grad_down, grad_up)


def solution(mesh):
    return jax.shard_map(
        on_device,
        mesh=mesh,
        in_specs=(
            P("dp", "seq", None),
            P("dp", "seq", None),
            P("dp", "seq", None),
            P("dp", "seq", None),
            P("dp", None),
            P("seq", None),
            P(),
            P(),
            P("dp", "seq", None),
            P("dp"),
        ),
        out_specs=(P("dp", "seq", None), P(), P()),
        check_vma=False,
    )
```

profile of v0, /device:TPU:10, one launch (start us, length us, event | category | flops | bytes accessed | tf_op | source)
XLA Modules:
  0.0 551.2 jit_solution(10076181569166712229)
XLA Ops:
  8.0 3.9 reshape_squeeze.12
  12.0 4.0 copy.35
  16.0 7.2 %all-to-all-start = ((bf16[192,16,2,128]{3,2,0,1:T(2,128)(2,1)}), bf16[192,16,2,128]{3,2,0,1:T(2,128)(2,1)}, u32[]{:S(2)}, u32[]{:S(2)}) async-start(bf16[192,16,2,128]{3,2,0,1:T(2,128)(2,1)} %copy.35), calls=%async_computation | async-start | bytes 3145728 | tf_op jit(solution)/shard_map/all_to_all | solution.py:62
  23.2 3.8 reshape_squeeze.14
  30.1 16.8 %all-to-all-done = bf16[192,16,2,128]{3,2,0,1:T(2,128)(2,1)} async-done(((bf16[192,16,2,128]{3,2,0,1:T(2,128)(2,1)}), bf16[192,16,2,128]{3,2,0,1:T(2,128)(2,1)}, u32[]{:S(2)}, u32[]{:S(2)}) %all-to-all-start) | async-done | bytes 1572896 | tf_op jit(solution)/shard_map/all_to_all | solution.py:62
  47.0 4.4 all-to-all-start.1
  51.4 3.8 reshape_squeeze.15
  55.2 3.2 copy.39
  58.4 16.8 %all-to-all-done.1 = bf16[192,16,2,128]{3,0,2,1:T(8,128)(2,1)} async-done(((bf16[192,16,2,128]{3,0,2,1:T(8,128)(2,1)}), bf16[192,16,2,128]{3,0,2,1:T(8,128)(2,1)}, u32[]{:S(2)}, u32[]{:S(2)}) %all-to-all-start.1) | async-done | bytes 1572896 | tf_op jit(solution)/shard_map/all_to_all | solution.py:63
  75.2 4.4 all-to-all-start.2
  85.4 17.9 %all-to-all-done.2 = bf16[192,16,2,128]{3,0,2,1:T(8,128)(2,1)} async-done(((bf16[192,16,2,128]{3,0,2,1:T(8,128)(2,1)}), bf16[192,16,2,128]{3,0,2,1:T(8,128)(2,1)}, u32[]{:S(2)}, u32[]{:S(2)}) %all-to-all-start.2) | async-done | bytes 1572896 | tf_op jit(solution)/shard_map/all_to_all | solution.py:64
  106.0 109.0 %while.11 = (s32[]{:T(128)}, bf16[6,512,2,128]{3,1,2,0:T(8,128)(2,1)}, bf16[6,512,2,128]{3,1,0,2:T(8,128)(2,1)}, bf16[3072,2,128]{2,0,1:T(8,128)(2,1)}, bf16[3072,2,128]{2,0,1:T(8,128)(2,1)}, /*index=5*/s32[]{:T(128)}, s32[]{:T(128)}) while((s32[]{:T(128)}, bf16[6,512,2,128]{3,1,2,0:T(8,128)(2,1)}, ...), condition=%wide.region_3.4_spmd.clone, body=%wide.region_0.3_spmd.clone.sunk | while | flops 1629624320 | bytes 28850272 | solution.py:31
  106.7 10.0 %fusion.71 = (f32[2,512]{1,0:T(2,128)S(1)}, f32[2,512,3072]{2,1,0:T(8,128)}) fusion(pred[3072]{0:T(1024)(128)(4,1)S(1)} %iota_compare_fusion.2, bf16[3072,2,128]{2,0,1:T(8,128)(2,1)} %get-tuple-element.149, bf16[6,512,2,128]{3,1,0,2:T(8,128)(2,1)} %get-tuple-element.148, s32[]{:T(128)S(6)} %copy.57), kind=kOutput, calls=%fused_computation.40.clone.1 | convolution fusion | flops 817892352 | bytes 14425092 | tf_op jit(solution)/shard_map/while/body/eval_jaxpr/sub | solution.py:25
  116.7 7.5 %fusion.72 = bf16[6,512,2,128]{3,1,2,0:T(8,128)(2,1)} fusion(bf16[6,512,2,128]{3,1,2,0:T(8,128)(2,1)} %get-tuple-element.140, s32[]{:T(128)S(6)} %copy.57, bf16[3072,2,128]{2,0,1:T(8,128)(2,1)} %get-tuple-element.150, f32[2,512,3072]{2,1,0:T(8,128)} %get-tuple-element.130, f32[2,512]{1,0:T(2,128)S(1)} %get-tuple-element.131), kind=kOutput, calls=%fused_computation.13.clone.1 | convolution fusion | flops 811728896 | bytes 14422020 | tf_op jit(solution)/shard_map/while/body/eval_jaxpr/hqk,khe->qhe/dot_general | solution.py:27
  124.9 10.0 %fusion.71 = (f32[2,512]{1,0:T(2,128)S(1)}, f32[2,512,3072]{2,1,0:T(8,128)}) fusion(pred[3072]{0:T(1024)(128)(4,1)S(1)} %iota_compare_fusion.2, bf16[3072,2,128]{2,0,1:T(8,128)(2,1)} %get-tuple-element.149, bf16[6,512,2,128]{3,1,0,2:T(8,128)(2,1)} %get-tuple-element.148, s32[]{:T(128)S(6)} %copy.57), kind=kOutput, calls=%fused_computation.40.clone.1 | convolution fusion | flops 817892352 | bytes 14425092 | tf_op jit(solution)/shard_map/while/body/eval_jaxpr/sub | solution.py:25
  134.8 7.5 %fusion.72 = bf16[6,512,2,128]{3,1,2,0:T(8,128)(2,1)} fusion(bf16[6,512,2,128]{3,1,2,0:T(8,128)(2,1)} %get-tuple-element.140, s32[]{:T(128)S(6)} %copy.57, bf16[3072,2,128]{2,0,1:T(8,128)(2,1)} %get-tuple-element.150, f32[2,512,3072]{2,1,0:T(8,128)} %get-tuple-element.130, f32[2,512]{1,0:T(2,128)S(1)} %get-tuple-element.131), kind=kOutput, calls=%fused_computation.13.clone.1 | convolution fusion | flops 811728896 | bytes 14422020 | tf_op jit(solution)/shard_map/while/body/eval_jaxpr/hqk,khe->qhe/dot_general | solution.py:27
  143.0 10.0 %fusion.71 = (f32[2,512]{1,0:T(2,128)S(1)}, f32[2,512,3072]{2,1,0:T(8,128)}) fusion(pred[3072]{0:T(1024)(128)(4,1)S(1)} %iota_compare_fusion.2, bf16[3072,2,128]{2,0,1:T(8,128)(2,1)} %get-tuple-element.149, bf16[6,512,2,128]{3,1,0,2:T(8,128)(2,1)} %get-tuple-element.148, s32[]{:T(128)S(6)} %copy.57), kind=kOutput, calls=%fused_computation.40.clone.1 | convolution fusion | flops 817892352 | bytes 14425092 | tf_op jit(solution)/shard_map/while/body/eval_jaxpr/sub | solution.py:25
  153.0 7.5 %fusion.72 = bf16[6,512,2,128]{3,1,2,0:T(8,128)(2,1)} fusion(bf16[6,512,2,128]{3,1,2,0:T(8,128)(2,1)} %get-tuple-element.140, s32[]{:T(128)S(6)} %copy.57, bf16[3072,2,128]{2,0,1:T(8,128)(2,1)} %get-tuple-element.150, f32[2,512,3072]{2,1,0:T(8,128)} %get-tuple-element.130, f32[2,512]{1,0:T(2,128)S(1)} %get-tuple-element.131), kind=kOutput, calls=%fused_computation.13.clone.1 | convolution fusion | flops 811728896 | bytes 14422020 | tf_op jit(solution)/shard_map/while/body/eval_jaxpr/hqk,khe->qhe/dot_general | solution.py:27
  161.2 10.0 %fusion.71 = (f32[2,512]{1,0:T(2,128)S(1)}, f32[2,512,3072]{2,1,0:T(8,128)}) fusion(pred[3072]{0:T(1024)(128)(4,1)S(1)} %iota_compare_fusion.2, bf16[3072,2,128]{2,0,1:T(8,128)(2,1)} %get-tuple-element.149, bf16[6,512,2,128]{3,1,0,2:T(8,128)(2,1)} %get-tuple-element.148, s32[]{:T(128)S(6)} %copy.57), kind=kOutput, calls=%fused_computation.40.clone.1 | convolution fusion | flops 817892352 | bytes 14425092 | tf_op jit(solution)/shard_map/while/body/eval_jaxpr/sub | solution.py:25
  171.2 7.5 %fusion.72 = bf16[6,512,2,128]{3,1,2,0:T(8,128)(2,1)} fusion(bf16[6,512,2,128]{3,1,2,0:T(8,128)(2,1)} %get-tuple-element.140, s32[]{:T(128)S(6)} %copy.57, bf16[3072,2,128]{2,0,1:T(8,128)(2,1)} %get-tuple-element.150, f32[2,512,3072]{2,1,0:T(8,128)} %get-tuple-element.130, f32[2,512]{1,0:T(2,128)S(1)} %get-tuple-element.131), kind=kOutput, calls=%fused_computation.13.clone.1 | convolution fusion | flops 811728896 | bytes 14422020 | tf_op jit(solution)/shard_map/while/body/eval_jaxpr/hqk,khe->qhe/dot_general | solution.py:27
  179.3 10.0 %fusion.71 = (f32[2,512]{1,0:T(2,128)S(1)}, f32[2,512,3072]{2,1,0:T(8,128)}) fusion(pred[3072]{0:T(1024)(128)(4,1)S(1)} %iota_compare_fusion.2, bf16[3072,2,128]{2,0,1:T(8,128)(2,1)} %get-tuple-element.149, bf16[6,512,2,128]{3,1,0,2:T(8,128)(2,1)} %get-tuple-element.148, s32[]{:T(128)S(6)} %copy.57), kind=kOutput, calls=%fused_computation.40.clone.1 | convolution fusion | flops 817892352 | bytes 14425092 | tf_op jit(solution)/shard_map/while/body/eval_jaxpr/sub | solution.py:25
  189.3 7.5 %fusion.72 = bf16[6,512,2,128]{3,1,2,0:T(8,128)(2,1)} fusion(bf16[6,512,2,128]{3,1,2,0:T(8,128)(2,1)} %get-tuple-element.140, s32[]{:T(128)S(6)} %copy.57, bf16[3072,2,128]{2,0,1:T(8,128)(2,1)} %get-tuple-element.150, f32[2,512,3072]{2,1,0:T(8,128)} %get-tuple-element.130, f32[2,512]{1,0:T(2,128)S(1)} %get-tuple-element.131), kind=kOutput, calls=%fused_computation.13.clone.1 | convolution fusion | flops 811728896 | bytes 14422020 | tf_op jit(solution)/shard_map/while/body/eval_jaxpr/hqk,khe->qhe/dot_general | solution.py:27
  197.5 10.0 %fusion.71 = (f32[2,512]{1,0:T(2,128)S(1)}, f32[2,512,3072]{2,1,0:T(8,128)}) fusion(pred[3072]{0:T(1024)(128)(4,1)S(1)} %iota_compare_fusion.2, bf16[3072,2,128]{2,0,1:T(8,128)(2,1)} %get-tuple-element.149, bf16[6,512,2,128]{3,1,0,2:T(8,128)(2,1)} %get-tuple-element.148, s32[]{:T(128)S(6)} %copy.57), kind=kOutput, calls=%fused_computation.40.clone.1 | convolution fusion | flops 817892352 | bytes 14425092 | tf_op jit(solution)/shard_map/while/body/eval_jaxpr/sub | solution.py:25
  207.5 7.5 %fusion.72 = bf16[6,512,2,128]{3,1,2,0:T(8,128)(2,1)} fusion(bf16[6,512,2,128]{3,1,2,0:T(8,128)(2,1)} %get-tuple-element.140, s32[]{:T(128)S(6)} %copy.57, bf16[3072,2,128]{2,0,1:T(8,128)(2,1)} %get-tuple-element.150, f32[2,512,3072]{2,1,0:T(8,128)} %get-tuple-element.130, f32[2,512]{1,0:T(2,128)S(1)} %get-tuple-element.131), kind=kOutput, calls=%fused_computation.13.clone.1 | convolution fusion | flops 811728896 | bytes 14422020 | tf_op jit(solution)/shard_map/while/body/eval_jaxpr/hqk,khe->qhe/dot_general | solution.py:27
  218.1 13.8 %convolution_convert_fusion = bf16[3072,5120]{1,0:T(8,128)(2,1)} fusion(bf16[256,5120]{1,0:T(8,128)(2,1)S(1)} %copy-done, bf16[384,8,2,128]{3,2,1,0:T(2,128)(2,1)S(1)} %bitcast.81), kind=kOutput, calls=%fused_computation.24 | convolution fusion | flops 8068792320 | bytes 35651584 | tf_op jit(solution)/shard_map/dot_general | solution.py:81
  233.4 13.4 %copy.44 = bf16[3072,2,128]{2,1,0:T(2,128)(2,1)S(1)} copy(bf16[3072,2,128]{2,0,1:T(8,128)(2,1)S(1)} %bitcast.82) | data formatting | bytes 3145728 | tf_op jit(solution)/shard_map/squeeze;broadcast_in_dim;reshape | solution.py:70
  246.8 26.3 %all_to_all.60 = bf16[3072,2,128]{2,1,0:T(2,128)(2,1)S(1)} all-to-all(bf16[3072,2,128]{2,1,0:T(2,128)(2,1)S(1)} %copy.44), channel_id=1, replica_groups=mesh['dp'=8,'seq'=16] {'seq'}, dimensions={0} | all-to-all | bytes 3145728 | tf_op jit(solution)/shard_map/all_to_all | solution.py:35
  275.3 3.9 reshape.20
  283.0 4.4 fusion.45
  287.4 170.4 %reduce-scatter.2.cloned.1.call-done = bf16[192,5120]{1,0:T(8,128)(2,1)} async-done(((bf16[3072,5120]{1,0:T(8,128)(2,1)}), bf16[192,5120]{1,0:T(8,128)(2,1)}) %reduce-scatter.2.cloned.1.call-update) | async-done | bytes 1966096 | tf_op jit(solution)/shard_map/reduce_scatter | solution.py:80
  457.9 4.4 fusion.33
  462.3 78.1 %all-reduce.3.cloned.1.call-done = (f32[4096,64]{0,1:T(8,128)}, f32[64,5120]{1,0:T(8,128)}) async-done(((f32[4096,64]{0,1:T(8,128)}, f32[64,5120]{1,0:T(8,128)}), (f32[4096,64]{0,1:T(8,128)}, f32[64,5120]{1,0:T(8,128)})) %all-reduce.3.cloned.1.call-update) | async-done | bytes 2359312 | tf_op jit(solution)/shard_map/psum | solution.py:96
  (34 shorter events, 29.6 us)
Async XLA Ops:
  8.0 210.1 %copy-start = (bf16[256,5120]{1,0:T(8,128)(2,1)S(1)}, bf16[256,5120]{1,0:T(8,128)(2,1)}, u32[]{:S(2)}) copy-start(bf16[256,5120]{1,0:T(8,128)(2,1)} %param.17) | copy-start | bytes 7864324
  16.0 31.0 %all-to-all-start = ((bf16[192,16,2,128]{3,2,0,1:T(2,128)(2,1)}), bf16[192,16,2,128]{3,2,0,1:T(2,128)(2,1)}, u32[]{:S(2)}, u32[]{:S(2)}) async-start(bf16[192,16,2,128]{3,2,0,1:T(2,128)(2,1)} %copy.35), calls=%async_computation | async-start | bytes 3145728 | tf_op jit(solution)/shard_map/all_to_all | solution.py:62
  47.0 28.2 %all-to-all-start.1 = ((bf16[192,16,2,128]{3,0,2,1:T(8,128)(2,1)}), bf16[192,16,2,128]{3,0,2,1:T(8,128)(2,1)}, u32[]{:S(2)}, u32[]{:S(2)}) async-start(bf16[192,16,2,128]{3,0,2,1:T(8,128)(2,1)} %copy.37), calls=%async_computation.1 | async-start | bytes 3145728 | tf_op jit(solution)/shard_map/all_to_all | solution.py:63
  75.2 28.2 %all-to-all-start.2 = ((bf16[192,16,2,128]{3,0,2,1:T(8,128)(2,1)}), bf16[192,16,2,128]{3,0,2,1:T(8,128)(2,1)}, u32[]{:S(2)}, u32[]{:S(2)}) async-start(bf16[192,16,2,128]{3,0,2,1:T(8,128)(2,1)} %copy.39), calls=%async_computation.2 | async-start | bytes 3145728 | tf_op jit(solution)/shard_map/all_to_all | solution.py:64
  79.6 378.3 %reduce-scatter.2.cloned.1.call-start = ((), (), s32[]{:S(2)}) async-start(), calls=%async_computation.5 | async-start | bytes 33423360 | tf_op jit(solution)/shard_map/reduce_scatter | solution.py:80
  231.8 308.5 %all-reduce.3.cloned.1.call-start = ((), (), s32[]{:S(2)}) async-start(), calls=%async_computation.6 | async-start | bytes 4718592 | tf_op jit(solution)/shard_map/psum | solution.py:96
  275.3 3.9 copy-start.4
  275.3 6.1 %copy-start.5 = (f32[1,5120]{1,0:T(1,128)S(1)}, f32[1,5120]{1,0:T(1,128)}, u32[]{:S(2)}) copy-start(f32[1,5120]{1,0:T(1,128)} %param.16) | copy-start | bytes 61444
  279.2 2.2 copy-start.1
  281.4 1.6 copy-start.2
  540.3 2.4 copy-start.3
Sparse Core Ops, SparseCore 0:
  232.0 225.8 reduce-scatter.1
Sparse Core Ops, SparseCore 1:
  287.5 252.8 all-reduce.2
where the time goes:
time: 554 us; the launch traced here: 551 us
  waiting for transfers between devices  300 us (54%)
  matrix products  131 us (24%)
  local copies, waits for them, and re-layouts  57.7 us (10%)
  blocking collectives  26.3 us (5%)
  starting transfers between devices  16.3 us (3%)
  between operations  15.6 us (3%)
    reduce_scatter x1, waiting for transfers between devices, on_device(): lax.psum_scatter(jnp.dot(head_rows, out_weight, preferred_element_type=jn...  170 us
    psum x1, waiting for transfers between devices, on_device(): grad_down, grad_up = lax.psum((down_part, up_part), ('dp', 'seq'))  78.1 us
    sub x6, matrix products, one_block(): powers = jnp.exp(scores - largest)  59.9 us
    dot_general x6, matrix products, one_block(): jnp.einsum('hqk,khe->qhe', weights, value_part, preferred_element_type=jn...  45.2 us
    all_to_all x1, blocking collectives, to_tokens(): lax.all_to_all(head_mixed, 'seq', split_axis=0, concat_axis=1, tiled=True)  26.3 us
    another operation x6, local copies, waits for them, and re-layouts, split_heads(): return matrix_in[0].reshape(tokens, groups, group_heads, HEAD_DIM)  21.9 us
    all_to_all x1, waiting for transfers between devices, on_device(): lax.all_to_all(split_heads(value_rows), 'seq', split_axis=1, concat_axis=...  17.9 us
    all_to_all x1, waiting for transfers between devices, on_device(): lax.all_to_all(split_heads(queries), 'seq', split_axis=1, concat_axis=0,...  16.8 us
  transfers between devices with their start and end apart: 5, of which 5 were waited for; matrix products, arithmetic and copies ran while one was open for 10% of the time, Pallas kernels for 0%

commit v1 on v0

v1 whole, which is shorter than its diff:
```python
import jax
import jax.numpy as jnp
import numpy as np
from jax import lax
from jax.experimental import pallas as pl
from jax.experimental.pallas import tpu as pltpu
from jax.sharding import Mesh
from jax.sharding import PartitionSpec as P

AXES = ("x", "yl", "z", "yh", "c")
DP = ("x", "yl")
SEQ = ("z", "yh", "c")
MESH = pl.DeviceIdType.MESH
HEAD = 128
RANK = 64
TOK = 192
CHIP = 2 * TOK
SEQLEN = 3072
D = 5120
QUARTER = D // 4
BQ = 768
KC = 512
SCALE = float(HEAD**-0.5 * np.log2(np.e))
F32 = jnp.float32
BF16 = jnp.bfloat16


def kernel(
    len_ref, q, k, v, res, gate, w, down, up, cot,
    out, gd, gu,
    qkv, bias, att, ag, wq, lg, dn, low, ps, pk, pr, yb,
    gdp, gup, l0, l1, g0, gs, g1, g2u, g2d, gda,
    snd, qkv_sem, lg_sem, ag_sem, wq_sem, fwd_sem, lr_sem, g0_sem, g1_sem, g2u_sem, g2d_sem, g3_sem, g4_sem, pr_sem, yb_sem,
):
    x, yl, z, yh, c = (lax.axis_index(a) for a in AXES)
    s = z * 4 + yh * 2 + c
    j = z * 2 + yh
    dp = x * 2 + yl
    own = pl.ds(s * TOK, TOK)

    def seq_peer(p):
        return {"z": p // 4, "yh": lax.rem(p, 4) // 2, "c": lax.rem(p, 2)}

    def chip_peer(p):
        return {"z": p // 2, "yh": lax.rem(p, 2)}

    def dp_peer(p):
        return {"x": p // 2, "yl": lax.rem(p, 2)}

    other = {"c": 1 - c}

    def remote(src, dst, sem, dev):
        return pltpu.make_async_remote_copy(
            src_ref=src, dst_ref=dst, send_sem=snd, recv_sem=sem, device_id=dev, device_id_type=MESH
        )

    def landed(ref, sem):
        pltpu.make_async_copy(ref, ref, sem).wait()

    barrier = pltpu.get_barrier_semaphore()

    def greet_seq(d, _):
        pl.semaphore_signal(barrier, inc=1, device_id=seq_peer(lax.rem(s + d, 16)), device_id_type=MESH)
        return 0

    def greet_dp(d, _):
        pl.semaphore_signal(barrier, inc=1, device_id=dp_peer(lax.rem(dp + d, 8)), device_id_type=MESH)
        return 0

    lax.fori_loop(1, 16, greet_seq, 0)
    lax.fori_loop(1, 8, greet_dp, 0)
    pl.semaphore_wait(barrier, 22)

    def send_head(h):
        def columns(p):
            return pl.ds(pl.multiple_of(p * 256 + h * HEAD, HEAD), HEAD)

        for a, src in enumerate((q, k, v)):
            pltpu.make_async_copy(src.at[:, columns(s)], qkv.at[h, a, own], qkv_sem.at[h]).start()

        def step(d, _):
            p = lax.rem(s + d, 16)
            for a, src in enumerate((q, k, v)):
                remote(src.at[:, columns(p)], qkv.at[h, a, own], qkv_sem.at[h], seq_peer(p)).start()
            return 0

        lax.fori_loop(1, 16, step, 0)

    send_head(0)

    bias[...] = jnp.where(lax.broadcasted_iota(jnp.int32, (SEQLEN, HEAD), 0) < len_ref[0], 0.0, -1e30)
    def scaled(cols):
        return (cot[:, cols].astype(F32) * gate[:, cols]).astype(BF16)

    low_grad = jnp.zeros((TOK, RANK), F32)
    for t in range(5):
        cols = slice(t * 1024, (t + 1) * 1024)
        low_grad += lax.dot_general(scaled(cols), up[:, cols], (((1,), (1,)), ((), ())), preferred_element_type=F32)
    lg[own, :] = jnp.zeros((TOK, HEAD), BF16)
    lg[own, 0:RANK] = low_grad.astype(BF16)

    def send_low_grad(d, _):
        remote(lg.at[own], lg.at[own], lg_sem, seq_peer(lax.rem(s + d, 16))).start()
        return 0

    lax.fori_loop(1, 16, send_low_grad, 0)

    for h in range(2):
        for t in range(8):
            dn[h, t * HEAD : (t + 1) * HEAD, :] = down[pl.ds(512 * t + 256 * c + 128 * h, HEAD), :]

    def attend(h):
        def chunk(i, total):
            zz = lax.rem(z + 1 + i, 4)
            rows = pl.ds(pl.multiple_of(zz * BQ, BQ), BQ)
            queries = qkv[h, 0, rows, :]
            scores, top = [], None
            for t in range(SEQLEN // KC):
                keys = slice(t * KC, (t + 1) * KC)
                part = lax.dot_general(qkv[h, 1, keys, :], queries, (((1,), (1,)), ((), ())), preferred_element_type=F32)
                part = part + jnp.concatenate([bias[keys, :]] * (BQ // HEAD), 1)
                scores.append(part)
                largest = jnp.max(part, axis=0, keepdims=True)
                top = largest if top is None else jnp.maximum(top, largest)
            top = top * SCALE
            mixed, weight = None, None
            for t in range(SEQLEN // KC):
                keys = slice(t * KC, (t + 1) * KC)
                powers = jnp.exp2(scores[t] * SCALE - top)
                summed = jnp.sum(powers, axis=0, keepdims=True)
                product = lax.dot_general(
                    qkv[h, 2, keys, :], powers.astype(BF16), (((0,), (0,)), ((), ())), preferred_element_type=F32
                )
                mixed = product if mixed is None else mixed + product
                weight = summed if weight is None else weight + summed
            mixed = mixed / weight
            att[h, rows, :] = mixed.T.astype(BF16)

            def piece(yy):
                src = att.at[h, pl.ds(pl.multiple_of(zz * BQ + yy * CHIP, CHIP), CHIP), :]
                return src, ag.at[h, x, :, pl.ds(pl.multiple_of(j * HEAD, HEAD), HEAD)]

            src, dst = piece(1 - yh)
            remote(src, dst, ag_sem.at[h], chip_peer(zz * 2 + 1 - yh)).start()
            src, dst = piece(yh)

            @pl.when(i < 3)
            def _():
                remote(src, dst, ag_sem.at[h], chip_peer(zz * 2 + yh)).start()

            @pl.when(i == 3)
            def _():
                pltpu.make_async_copy(src, dst, ag_sem.at[h]).start()

            return total + jnp.dot(mixed.astype(BF16), lg[rows, :], preferred_element_type=F32)

        gdp[h * HEAD : (h + 1) * HEAD, :] = lax.fori_loop(0, SEQLEN // BQ, chunk, jnp.zeros((HEAD, HEAD), F32))

    landed(qkv.at[0], qkv_sem.at[0])
    send_head(1)
    landed(lg.at[pl.ds(0, 15 * TOK)], lg_sem)
    attend(0)
    landed(qkv.at[1], qkv_sem.at[1])

    def weight_piece(h):
        src = w.at[pl.ds(h * HEAD, HEAD), pl.ds(pl.multiple_of(x * QUARTER, QUARTER), QUARTER)]
        return src, wq.at[h, pl.ds(pl.multiple_of(j * HEAD, HEAD), HEAD), :]

    for h in range(2):
        src, dst = weight_piece(h)
        pltpu.make_async_copy(src, dst, wq_sem).start()

        def send_weight(d, _):
            remote(src, dst, wq_sem, chip_peer(lax.rem(j + d, 8))).start()
            return 0

        lax.fori_loop(1, 8, send_weight, 0)

    def forward(h):
        landed(ag.at[h, x], ag_sem.at[h])

        def step(d, _):
            remote(ag.at[h, x], ag.at[h, x], fwd_sem.at[h, x], {"x": lax.rem(x + d, 4)}).start()
            return 0

        lax.fori_loop(1, 4, step, 0)

    forward(0)
    attend(1)
    forward(1)

    l0[...] = jnp.zeros((CHIP, HEAD), F32)
    l0[:, 0:RANK] = jnp.dot(ag[0, x], dn[0], preferred_element_type=F32) + jnp.dot(ag[1, x], dn[1], preferred_element_type=F32)
    remote(l0.at[pl.ds((1 - c) * TOK, TOK)], l1, lr_sem, other).start()
    landed(l1, lr_sem)
    low[...] = (l0[pl.ds(c * TOK, TOK), 0:RANK] + l1[:, 0:RANK]).astype(BF16)

    for t in range(5):
        cols = slice(t * 1024, (t + 1) * 1024)
        gup[:, cols] = lax.dot_general(low[...], scaled(cols), (((0,), (0,)), ((), ())), preferred_element_type=F32)
    remote(gup.at[pl.ds((1 - c) * 32, 32)], g0, g0_sem, other).start()
    landed(g0, g0_sem)
    gs[...] = gup[pl.ds(c * 32, 32), :] + g0[...]

    def columns640(p):
        return pl.ds(pl.multiple_of(p * 640, 640), 640)

    def reduce_up(d, _):
        p = lax.rem(j + d, 8)
        remote(gs.at[:, columns640(p)], g1.at[j], g1_sem, chip_peer(p)).start()
        return 0

    lax.fori_loop(1, 8, reduce_up, 0)
    pltpu.make_async_copy(gs.at[:, columns640(j)], g1.at[j], g1_sem).start()
    landed(g1, g1_sem)
    total = g1[0]
    for t in range(1, 8):
        total = total + g1[t]
    g2u[dp] = total
    g2d[dp] = gdp[...]

    def over_clips(d, _):
        dev = dp_peer(lax.rem(dp + d, 8))
        remote(g2u.at[dp], g2u.at[dp], g2u_sem, dev).start()
        remote(g2d.at[dp], g2d.at[dp], g2d_sem, dev).start()
        return 0

    lax.fori_loop(1, 8, over_clips, 0)
    landed(g2u.at[pl.ds(0, 7)], g2u_sem)
    landed(g2d.at[pl.ds(0, 7)], g2d_sem)
    total = g2u[0]
    total_down = g2d[0]
    for t in range(1, 8):
        total = total + g2u[t]
        total_down = total_down + g2d[t]
    g0[:, 0:640] = total
    rank_rows = pl.ds(pl.multiple_of(c * 32, 32), 32)
    up_piece = gu.at[rank_rows, columns640(j)]
    gda[c, j] = total_down
    pltpu.make_async_copy(g0.at[:, 0:640], up_piece, g3_sem.at[0]).start()

    def spread(d, _):
        dev = chip_peer(lax.rem(j + d, 8))
        remote(g0.at[:, 0:640], up_piece, g3_sem.at[0], dev).start()
        remote(gda.at[c, j], gda.at[c, j], g4_sem.at[0], dev).start()
        return 0

    lax.fori_loop(1, 8, spread, 0)

    landed(wq, wq_sem)
    for d in range(4):
        xx = lax.rem(x + 4 - d, 4)
        if d:
            for h in range(2):
                landed(ag.at[h, xx], fwd_sem.at[h, xx])

        def block(t, _):
            cols = pl.ds(pl.multiple_of(t * 256, 256), 256)
            part = jnp.dot(ag[0, xx], wq[0, :, cols], preferred_element_type=F32)
            part += jnp.dot(ag[1, xx], wq[1, :, cols], preferred_element_type=F32)
            first, second = part[:TOK], part[TOK:]
            pk[d, :, cols] = jnp.where(c == 0, first, second).astype(BF16)
            ps[d, :, cols] = jnp.where(c == 0, second, first).astype(BF16)
            return 0

        lax.fori_loop(0, QUARTER // 256, block, 0)
        remote(ps.at[d], pr.at[d], pr_sem.at[d], other).start()

    for d in range(4):
        landed(pr.at[d], pr_sem.at[d])
        pk[d] = (pk[d].astype(F32) + pr[d].astype(F32)).astype(BF16)
        if d:
            remote(pk.at[d], yb.at[x], yb_sem.at[x], {"x": lax.rem(x + 4 - d, 4)}).start()

    landed(gu.at[pl.ds(0, 32)], g3_sem.at[0])
    landed(gda.at[0, pl.ds(0, 7)], g4_sem.at[0])
    remote(gu.at[rank_rows], gu.at[rank_rows], g3_sem.at[1], other).start()
    remote(gda.at[c], gda.at[c], g4_sem.at[1], other).start()

    for d in range(4):
        xx = lax.rem(x + d, 4)
        if d:
            landed(yb.at[xx], yb_sem.at[xx])
        cols = pl.ds(pl.multiple_of(xx * QUARTER, QUARTER), QUARTER)
        base = (yb[xx] if d else pk[0]).astype(F32)
        delta = jnp.dot(low[...], up[:, cols], preferred_element_type=F32)
        out[:, cols] = (res[:, cols].astype(F32) + gate[:, cols] * (base + delta)).astype(BF16)

    landed(gu.at[pl.ds(0, 32)], g3_sem.at[1])
    landed(gda.at[0], g4_sem.at[1])
    for cc in range(2):
        for t in range(8):
            gd[(2 * t + cc) * 256 : (2 * t + cc + 1) * 256, :] = gda[cc, t, :, 0:RANK]

    def drain(count, ref):
        def step(_, carry):
            landed(ref, snd)
            return carry

        lax.fori_loop(0, count, step, 0)

    drain(90, qkv.at[0, 0, pl.ds(0, TOK)])
    drain(15, lg.at[pl.ds(0, TOK)])
    drain(14, att.at[0, pl.ds(0, CHIP), :])
    drain(14, wq.at[0, pl.ds(0, HEAD), :])
    drain(6, ag.at[0, 0])
    drain(1, l1)
    drain(1, g0)
    drain(7, g1.at[0])
    drain(7, g2u.at[0])
    drain(7, g2d.at[0])
    drain(7, g1.at[0])
    drain(7, gda.at[0, 0])
    drain(4, ps.at[0])
    drain(3, pk.at[0])
    drain(1, gu.at[pl.ds(0, 32)])
    drain(1, gda.at[0])


def on_device(q, k, v, res, gate, w, down, up, cot, lengths):
    vmem = pl.BlockSpec(memory_space=pltpu.VMEM)
    hbm = pl.BlockSpec(memory_space=pl.ANY)
    dma = pltpu.SemaphoreType.DMA
    out, gd, gu = pl.pallas_call(
        kernel,
        out_shape=(
            jax.ShapeDtypeStruct((TOK, D), BF16),
            jax.ShapeDtypeStruct((4096, RANK), F32),
            jax.ShapeDtypeStruct((RANK, D), F32),
        ),
        in_specs=[pl.BlockSpec(memory_space=pltpu.SMEM), hbm, hbm, hbm, vmem, vmem, hbm, vmem, vmem, vmem],
        out_specs=(vmem, vmem, vmem),
        scratch_shapes=[
            pltpu.VMEM((2, 3, SEQLEN, HEAD), BF16),
            pltpu.VMEM((SEQLEN, HEAD), F32),
            pltpu.VMEM((2, SEQLEN, HEAD), BF16),
            pltpu.VMEM((2, 4, CHIP, 1024), BF16),
            pltpu.VMEM((2, 1024, QUARTER), BF16),
            pltpu.VMEM((SEQLEN, HEAD), BF16),
            pltpu.VMEM((2, 1024, RANK), BF16),
            pltpu.VMEM((TOK, RANK), BF16),
            pltpu.VMEM((4, TOK, QUARTER), BF16),
            pltpu.VMEM((4, TOK, QUARTER), BF16),
            pltpu.VMEM((4, TOK, QUARTER), BF16),
            pltpu.VMEM((4, TOK, QUARTER), BF16),
            pltpu.VMEM((256, HEAD), F32),
            pltpu.VMEM((RANK, D), F32),
            pltpu.VMEM((CHIP, HEAD), F32),
            pltpu.VMEM((TOK, HEAD), F32),
            pltpu.VMEM((32, D), F32),
            pltpu.VMEM((32, D), F32),
            pltpu.VMEM((8, 32, 640), F32),
            pltpu.VMEM((8, 32, 640), F32),
            pltpu.VMEM((8, 256, HEAD), F32),
            pltpu.VMEM((2, 8, 256, HEAD), F32),
            dma,
            dma((2,)),
            dma,
            dma((2,)),
            dma,
            dma((2, 4)),
            dma,
            dma,
            dma,
            dma,
            dma,
            dma((2,)),
            dma((2,)),
            dma((4,)),
            dma((4,)),
        ],
        compiler_params=pltpu.CompilerParams(collective_id=1, has_side_effects=True, vmem_limit_bytes=63 * 2**20),
        cost_estimate=pl.CostEstimate(flops=18 * 10**9, bytes_accessed=30 * 10**6, transcendentals=19 * 10**6),
    )(lengths, q[0], k[0], v[0], res[0], gate, w, down, up, cot[0])
    return out[None], gd, gu


def solution(mesh):
    inner = Mesh(mesh.devices.reshape(4, 2, 4, 2, 2), AXES)
    return jax.shard_map(
        on_device,
        mesh=inner,
        in_specs=(
            P(DP, SEQ, None),
            P(DP, SEQ, None),
            P(DP, SEQ, None),
            P(DP, SEQ, None),
            P(DP, None),
            P(SEQ, None),
            P(),
            P(),
            P(DP, SEQ, None),
            P(DP),
        ),
        out_specs=(P(DP, SEQ, None), P(), P()),
        check_vma=False,
    )
```

time: 554 us -> 256 us (0.46)
  waiting for transfers between devices: 300 us -> 0 us
  Pallas kernels: 0 us -> 243 us
  matrix products: 131 us -> 0 us
  local copies, waits for them, and re-layouts: 57.7 us -> 8.73 us
  blocking collectives: 26.3 us -> 0 us
  starting transfers between devices: 16.3 us -> 0 us
  between operations: 15.6 us -> 1.3 us
    pallas_call x0 -> x1, Pallas kernels: none -> 243 us  [on_device(): pl.pallas_call(kernel, out_shape=(jax.ShapeDtypeStruct((TOK, D), BF16), j...]
    reduce_scatter x1 -> x0, waiting for transfers between devices: 170 us -> none  [on_device(): lax.psum_scatter(jnp.dot(head_rows, out_weight, preferred_element_type=jn...]
    psum x1 -> x0, waiting for transfers between devices: 78.1 us -> none  [on_device(): grad_down, grad_up = lax.psum((down_part, up_part), ('dp', 'seq'))]
    dot_general x11 -> x0, matrix products: 71.5 us -> none  [the longest x6 45.2 us: one_block(): jnp.einsum('hqk,khe->qhe', weights, value_part, preferred_element_type=jn...]
    sub x6 -> x0, matrix products: 59.9 us -> none  [one_block(): powers = jnp.exp(scores - largest)]
    all_to_all x3 -> x0, waiting for transfers between devices: 51.6 us -> none  [the longest x1 17.9 us: on_device(): lax.all_to_all(split_heads(value_rows), 'seq', split_axis=1, concat_axis=...]
    another operation x7 -> x0, local copies, waits for them, and re-layouts: 35.3 us -> none  [the longest x6 21.9 us: split_heads(): return matrix_in[0].reshape(tokens, groups, group_heads, HEAD_DIM)]
    all_to_all x1 -> x0, blocking collectives: 26.3 us -> none  [to_tokens(): lax.all_to_all(head_mixed, 'seq', split_axis=0, concat_axis=1, tiled=True)]
  transfers between devices with their start and end apart: 5 -> 0, of which waited for: 5 -> 0; matrix products, arithmetic and copies ran while one was open for 10% -> 0% of each run, Pallas kernels for 0% -> 0%
where the time goes in v1:
time: 256 us; the launch traced here: 253 us
  Pallas kernels  243 us (95%)
  local copies, waits for them, and re-layouts  8.73 us (3%)
    pallas_call x1, Pallas kernels, on_device(): pl.pallas_call(kernel, out_shape=(jax.ShapeDtypeStruct((TOK, D), BF16), j...  243 us
    unnamed x8, local copies, waits for them, and re-layouts  8.73 us

profile of v1, /device:TPU:10, one launch (start us, length us, event | category | flops | bytes accessed | tf_op | source)
XLA Modules:
  0.0 252.9 jit_solution(12155998956438705937)
XLA Ops:
  1.3 2.4 copy.13.down
  3.6 242.9 %shard_map.121 = (bf16[192,5120]{1,0:T(8,128)(2,1)}, f32[4096,64]{1,0:T(8,128)}, f32[64,5120]{1,0:T(8,128)}) custom-call(s32[1]{0:T(128)S(6)} %copy.17.len_ref, bf16[192,4096]{1,0:T(8,128)(2,1)} %bitcast.9, bf16[192,4096]{1,0:T(8,128)(2,1)} %bitcast.10, bf16[192,4096]{1,0:T(8,128)(2,1)} %bitcast.11, bf16[192,5120]{1,0:T(8,128)(2,1)} %bitcast.7, ...), custom_call_target="tpu_custom_call" | custom-call | flops 17999998976 | bytes 30000000 | tf_op jit(solution)/shard_map/pallas_call | solution.py:324
  246.5 0.0 copy-start
  246.6 3.3 %copy.14 = f32[4096,64]{0,1:T(8,128)} copy(f32[4096,64]{1,0:T(8,128)} %get-tuple-element.10) | data formatting | bytes 2097152
  249.8 0.0 copy-done
  249.8 0.0 copy-start.1
  249.8 1.3 copy.18
  251.1 0.8 copy-done.1
  251.9 1.1 copy.19
Async XLA Ops:
  246.5 3.3 %copy-start = (bf16[192,5120]{1,0:T(8,128)(2,1)S(1)}, bf16[192,5120]{1,0:T(8,128)(2,1)}, u32[]{:S(2)}) copy-start(bf16[192,5120]{1,0:T(8,128)(2,1)} %get-tuple-element.6) | copy-start | bytes 5898244
  249.8 2.0 copy-start.1

commit v2 on v1

v2 whole, which is shorter than its diff:
```python
import jax
import jax.numpy as jnp
import numpy as np
from jax import lax
from jax.experimental import pallas as pl
from jax.experimental.pallas import tpu as pltpu
from jax.sharding import Mesh
from jax.sharding import PartitionSpec as P

AXES = ("x", "yl", "z", "yh", "c")
DP = ("x", "yl")
SEQ = ("z", "yh", "c")
MESH = pl.DeviceIdType.MESH
HEAD = 128
RANK = 64
TOK = 192
CHIP = 2 * TOK
SEQLEN = 3072
D = 5120
QUARTER = D // 4
BQ = 768
KC = 512
SCALE = float(HEAD**-0.5 * np.log2(np.e))
F32 = jnp.float32
BF16 = jnp.bfloat16


def kernel(
    len_ref, q, k, v, res_hbm, gate, w, down, up_hbm, cot_hbm,
    out, gd, gu,
    qkv, bias, att, ag, wq, lgc, dn, low, ps, pk, pr, yb,
    res, up, cot, gup, l0, l1, g0, gs, g1, gdq, g1d, g2u, g2d, g3u, gda,
    snd, load_sem, qkv_sem, lg_sem, ag_sem, wq_sem, wl_sem, f1_sem, f2_sem, lr_sem, g0_sem, g1_sem, g1d_sem, g2u_sem, g2d_sem,
    g3u_sem, g3d_sem, g4_sem, pr_sem, yb_sem,
):
    x, yl, z, yh, c = (lax.axis_index(a) for a in AXES)
    s = z * 4 + yh * 2 + c
    j = z * 2 + yh
    dp = x * 2 + yl
    right, left = lax.rem(x + 1, 4), lax.rem(x + 3, 4)
    own = pl.ds(s * TOK, TOK)
    pending = []

    def seq_peer(p):
        return {"z": p // 4, "yh": lax.rem(p, 4) // 2, "c": lax.rem(p, 2)}

    def chip_peer(p):
        return {"z": p // 2, "yh": lax.rem(p, 2)}

    def dp_peer(p):
        return {"x": p // 2, "yl": lax.rem(p, 2)}

    other = {"c": 1 - c}

    def remote(src, dst, sem, dev):
        return pltpu.make_async_remote_copy(
            src_ref=src, dst_ref=dst, send_sem=snd, recv_sem=sem, device_id=dev, device_id_type=MESH
        )

    def send(src, dst, sem, dev):
        remote(src, dst, sem, dev).start()
        pending.append((1, src))

    def send_all(count, start, sample):
        def step(d, _):
            start(d)
            return 0

        lax.fori_loop(1, count + 1, step, 0)
        pending.append((count, sample))

    def landed(ref, sem):
        pltpu.make_async_copy(ref, ref, sem).wait()

    def drain():
        for count, ref in pending:

            def step(_, carry):
                landed(ref, snd)
                return carry

            lax.fori_loop(0, count, step, 0)
        pending.clear()

    barrier = pltpu.get_barrier_semaphore()

    def greet_seq(d, _):
        pl.semaphore_signal(barrier, inc=1, device_id=seq_peer(lax.rem(s + d, 16)), device_id_type=MESH)
        return 0

    def greet_dp(d, _):
        pl.semaphore_signal(barrier, inc=1, device_id=dp_peer(lax.rem(dp + d, 8)), device_id_type=MESH)
        return 0

    lax.fori_loop(1, 16, greet_seq, 0)
    lax.fori_loop(1, 8, greet_dp, 0)
    loads = [
        pltpu.make_async_copy(src, dst, load_sem.at[n])
        for n, (src, dst) in enumerate(((cot_hbm, cot), (up_hbm, up), (res_hbm, res)))
    ]
    loads[0].start()
    loads[1].start()
    pl.semaphore_wait(barrier, 22)

    def send_head(h):
        def columns(p):
            return pl.ds(pl.multiple_of(p * 256 + h * HEAD, HEAD), HEAD)

        def start(d):
            p = lax.rem(s + d, 16)
            for a, src in enumerate((q, k, v)):
                remote(src.at[:, columns(p)], qkv.at[h, a, own], qkv_sem.at[h], seq_peer(p)).start()

        for a, src in enumerate((q, k, v)):
            pltpu.make_async_copy(src.at[:, columns(s)], qkv.at[h, a, own], qkv_sem.at[h]).start()
        send_all(15, start, qkv.at[0, 0, pl.ds(0, 3 * TOK)])

    send_head(0)
    loads[2].start()

    bias[...] = jnp.where(lax.broadcasted_iota(jnp.int32, (SEQLEN, HEAD), 0) < len_ref[0], 0.0, -1e30)
    loads[0].wait()
    loads[1].wait()

    def scaled(cols):
        return (cot[:, cols].astype(F32) * gate[:, cols]).astype(BF16)

    low_grad = jnp.zeros((TOK, RANK), F32)
    for t in range(5):
        cols = slice(t * 1024, (t + 1) * 1024)
        low_grad += lax.dot_general(scaled(cols), up[:, cols], (((1,), (1,)), ((), ())), preferred_element_type=F32)
    half_own = pl.ds(pl.multiple_of(c * TOK, TOK), TOK)
    lgc[half_own, :] = jnp.zeros((TOK, HEAD), BF16)
    lgc[half_own, 0:RANK] = low_grad.astype(BF16)
    send(lgc.at[half_own], lgc.at[half_own], lg_sem, other)

    for h in range(2):
        for t in range(8):
            dn[h, :, t * HEAD : (t + 1) * HEAD] = down[:, pl.ds(pl.multiple_of(512 * t + 256 * c + 128 * h, HEAD), HEAD)]

    drain()
    send_head(1)

    def attend(h, between):
        def chunk(i, carry):
            zz = lax.rem(z + 1 + i, 4)
            rows = pl.ds(pl.multiple_of(zz * BQ, BQ), BQ)
            queries = qkv[h, 0, rows, :]
            scores, top = [], None
            for t in range(SEQLEN // KC):
                keys = slice(t * KC, (t + 1) * KC)
                part = lax.dot_general(qkv[h, 1, keys, :], queries, (((1,), (1,)), ((), ())), preferred_element_type=F32)
                part = part + jnp.concatenate([bias[keys, :]] * (BQ // HEAD), 1)
                scores.append(part)
                largest = jnp.max(part, axis=0, keepdims=True)
                top = largest if top is None else jnp.maximum(top, largest)
            top = top * SCALE
            mixed, weight = None, None
            for t in range(SEQLEN // KC):
                keys = slice(t * KC, (t + 1) * KC)
                powers = jnp.exp2(scores[t] * SCALE - top)
                summed = jnp.sum(powers, axis=0, keepdims=True)
                product = lax.dot_general(
                    qkv[h, 2, keys, :], powers.astype(BF16), (((0,), (0,)), ((), ())), preferred_element_type=F32
                )
                mixed = product if mixed is None else mixed + product
                weight = summed if weight is None else weight + summed
            mixed = mixed / weight
            att[h, rows, :] = mixed.T.astype(BF16)

            def piece(yy):
                src = att.at[h, pl.ds(pl.multiple_of(zz * BQ + yy * CHIP, CHIP), CHIP), :]
                return src, ag.at[h, x, :, pl.ds(pl.multiple_of(j * HEAD, HEAD), HEAD)]

            src, dst = piece(1 - yh)
            remote(src, dst, ag_sem.at[h], chip_peer(zz * 2 + 1 - yh)).start()
            src, dst = piece(yh)

            @pl.when(i < 3)
            def _():
                remote(src, dst, ag_sem.at[h], chip_peer(zz * 2 + yh)).start()

            @pl.when(i == 3)
            def _():
                pltpu.make_async_copy(src, dst, ag_sem.at[h]).start()

            for when, action in between.items():
                pl.when(i == when)(action)
            return carry

        lax.fori_loop(0, SEQLEN // BQ, chunk, 0)
        pending.append((7, att.at[0, pl.ds(0, CHIP), :]))

    def piece_columns(n):
        return pl.ds(pl.multiple_of(n * 256, 256), 256)

    def send_weights(n, sem):
        for h in range(2):
            cols = pl.ds(pl.multiple_of(x * QUARTER + n * 256, 256), 256)
            src = w.at[pl.ds(h * HEAD, HEAD), cols]
            dst = wq.at[h, pl.ds(pl.multiple_of(j * HEAD, HEAD), HEAD), piece_columns(n)]
            pltpu.make_async_copy(src, dst, sem).start()
            send_all(
                7,
                lambda d, src=src, dst=dst: remote(src, dst, sem, chip_peer(lax.rem(j + d, 8))).start(),
                wq.at[0, pl.ds(0, HEAD), pl.ds(0, 256)],
            )

    def swap_weights():
        shared = wq.at[:, :, piece_columns(yl)]
        landed(shared, wq_sem.at[0])
        remote(shared, shared, wl_sem, {"yl": 1 - yl}).start()

    def forward(h):
        landed(ag.at[h, x], ag_sem.at[h])
        remote(ag.at[h, x], ag.at[h, x], f1_sem.at[h, 0], {"x": right}).start()
        remote(ag.at[h, x], ag.at[h, x], f1_sem.at[h, 1], {"x": left}).start()

    def forward_on(h):
        for n, (source, target) in enumerate(((left, right), (right, left))):
            landed(ag.at[h, source], f1_sem.at[h, n])
            half = ag.at[h, source, pl.ds(n * TOK, TOK)]
            send(half, half, f2_sem.at[h], {"x": target})

    landed(qkv.at[0], qkv_sem.at[0])
    attend(0, {})
    landed(qkv.at[1], qkv_sem.at[1])
    send_weights(yl, wq_sem.at[0])
    attend(1, {1: lambda: forward(0), 2: swap_weights})
    pending.append((2, ag.at[0, 0]))
    pending.append((1, wq.at[:, :, pl.ds(0, 256)]))
    send_weights(2, wq_sem.at[1])
    send_weights(3, wq_sem.at[2])

    forward_on(0)
    forward(1)
    pending.append((2, ag.at[0, 0]))

    l0[...] = jnp.zeros((CHIP, HEAD), F32)
    l0[:, 0:RANK] = lax.dot_general(
        ag[0, x], dn[0], (((1,), (1,)), ((), ())), preferred_element_type=F32
    ) + lax.dot_general(ag[1, x], dn[1], (((1,), (1,)), ((), ())), preferred_element_type=F32)
    send(l0.at[pl.ds((1 - c) * TOK, TOK)], l1, lr_sem, other)
    landed(l1, lr_sem)
    low[...] = (l0[pl.ds(c * TOK, TOK), 0:RANK] + l1[:, 0:RANK]).astype(BF16)

    for t in range(5):
        cols = slice(t * 1024, (t + 1) * 1024)
        gup[:, cols] = lax.dot_general(low[...], scaled(cols), (((0,), (0,)), ((), ())), preferred_element_type=F32).astype(BF16)
    send(gup.at[pl.ds((1 - c) * 32, 32)], g0, g0_sem, other)
    landed(g0, g0_sem)
    gs[...] = (gup[pl.ds(c * 32, 32), :].astype(F32) + g0[...].astype(F32)).astype(BF16)

    landed(lgc.at[pl.ds(0, TOK)], lg_sem)
    for h in range(2):
        gdq[h] = lax.dot_general(lgc[...], ag[h, x], (((0,), (0,)), ((), ())), preferred_element_type=F32)[0:RANK].astype(BF16)

    def columns640(p):
        return pl.ds(pl.multiple_of(p * 640, 640), 640)

    pltpu.make_async_copy(gs.at[:, columns640(j)], g1.at[j], g1_sem).start()
    send_all(
        7,
        lambda d: remote(gs.at[:, columns640(lax.rem(j + d, 8))], g1.at[j], g1_sem, chip_peer(lax.rem(j + d, 8))).start(),
        g1.at[0],
    )

    def head_columns(p):
        return pl.ds(pl.multiple_of(p * HEAD, HEAD), HEAD)

    pltpu.make_async_copy(gdq.at[:, :, head_columns(j)], g1d.at[j], g1d_sem).start()
    send_all(
        7,
        lambda d: remote(gdq.at[:, :, head_columns(lax.rem(j + d, 8))], g1d.at[j], g1d_sem, chip_peer(lax.rem(j + d, 8))).start(),
        g1d.at[0],
    )
    send_weights(4, wq_sem.at[3])
    forward_on(1)

    def total_of(ref):
        total = ref[0].astype(F32)
        for t in range(1, 8):
            total = total + ref[t].astype(F32)
        return total

    landed(g1, g1_sem)
    g2u[dp] = total_of(g1).astype(BF16)
    landed(g1d, g1d_sem)
    total = total_of(g1d)
    for h in range(2):
        g2d[dp, :, h * HEAD : (h + 1) * HEAD] = total[h].astype(BF16)
    send_all(
        7,
        lambda d: remote(g2d.at[dp], g2d.at[dp], g2d_sem, dp_peer(lax.rem(dp + d, 8))).start(),
        g2d.at[0],
    )
    send_all(
        7,
        lambda d: remote(g2u.at[dp], g2u.at[dp], g2u_sem, dp_peer(lax.rem(dp + d, 8))).start(),
        g2u.at[0],
    )

    groups = ((0, 3), (3, 2))

    def group_columns(g):
        first, count = groups[g]
        return pl.ds(first * 256, count * 256)

    def project(g, n, xx):
        def block(t, _):
            cols = piece_columns(t)
            part = jnp.dot(ag[0, xx], wq[0, :, cols], preferred_element_type=F32)
            part += jnp.dot(ag[1, xx], wq[1, :, cols], preferred_element_type=F32)
            first, second = part[:TOK], part[TOK:]
            pk[n, :, cols] = jnp.where(c == 0, first, second).astype(BF16)
            ps[n, :, cols] = jnp.where(c == 0, second, first).astype(BF16)
            return 0

        lax.fori_loop(groups[g][0], sum(groups[g]), block, 0)
        cols = group_columns(g)
        send(ps.at[n, :, cols], pr.at[n, :, cols], pr_sem.at[g, n], other)

    def finish(g, n, xx):
        cols = group_columns(g)
        landed(pr.at[n, :, cols], pr_sem.at[g, n])
        pk[n, :, cols] = (pk[n, :, cols].astype(F32) + pr[n, :, cols].astype(F32)).astype(BF16)
        if n:
            send(pk.at[n, :, cols], yb.at[x, :, cols], yb_sem.at[g, x], {"x": xx})

    far = lax.rem(x + 2, 4)

    def run_group(g):
        project(g, 1, right)
        project(g, 2, left)
        finish(g, 1, right)
        if g == 0:
            for h in range(2):
                landed(ag.at[h, far], f2_sem.at[h])
        project(g, 3, far)
        finish(g, 2, left)
        project(g, 0, x)
        finish(g, 3, far)
        finish(g, 0, x)

    landed(wq.at[:, :, pl.ds(0, 256)], wl_sem)
    landed(wq.at[:, :, pl.ds(0, 256)], wq_sem.at[1])
    run_group(0)

    landed(g2d.at[pl.ds(0, 7)], g2d_sem)
    gda[c, j] = total_of(g2d).astype(BF16)
    landed(g2u.at[pl.ds(0, 7)], g2u_sem)
    g3u[j] = total_of(g2u).astype(BF16)
    send_all(
        7,
        lambda d: remote(g3u.at[j], g3u.at[j], g3u_sem, chip_peer(lax.rem(j + d, 8))).start(),
        g3u.at[0],
    )
    send_all(
        7,
        lambda d: remote(gda.at[c, j], gda.at[c, j], g3d_sem, chip_peer(lax.rem(j + d, 8))).start(),
        gda.at[0, 0],
    )

    landed(wq.at[:, :, pl.ds(0, 256)], wq_sem.at[2])
    landed(wq.at[:, :, pl.ds(0, 256)], wq_sem.at[3])
    run_group(1)
    loads[2].wait()

    def write(g, base, xx):
        first, count = groups[g]
        cols = pl.ds(pl.multiple_of(xx * QUARTER + first * 256, 256), count * 256)
        delta = jnp.dot(low[...], up[:, cols], preferred_element_type=F32)
        out[:, cols] = (res[:, cols].astype(F32) + gate[:, cols] * (base.astype(F32) + delta)).astype(BF16)

    for g in range(2):
        write(g, pk[0, :, group_columns(g)], x)
    landed(g3u.at[pl.ds(0, 7)], g3u_sem)
    landed(gda.at[0, pl.ds(0, 7)], g3d_sem)
    send(g3u, g1, g4_sem.at[0], other)
    send(gda.at[c], gda.at[c], g4_sem.at[1], other)
    for g in range(2):
        for xx in (right, left, far):
            landed(yb.at[xx, :, group_columns(g)], yb_sem.at[g, xx])
            write(g, yb[xx, :, group_columns(g)], xx)
    landed(g1, g4_sem.at[0])
    landed(gda.at[0], g4_sem.at[1])
    rows_own, rows_other = (pl.ds(pl.multiple_of(r * 32, 32), 32) for r in (c, 1 - c))
    for t in range(8):
        gu[rows_own, t * 640 : (t + 1) * 640] = g3u[t].astype(F32)
        gu[rows_other, t * 640 : (t + 1) * 640] = g1[t].astype(F32)
        for cc in range(2):
            gd[:, (2 * t + cc) * 256 : (2 * t + cc + 1) * 256] = gda[cc, t].astype(F32)
    drain()


def on_device(q, k, v, res, gate, w, down, up, cot, lengths):
    vmem = pl.BlockSpec(memory_space=pltpu.VMEM)
    hbm = pl.BlockSpec(memory_space=pl.ANY)
    dma = pltpu.SemaphoreType.DMA
    out, gd, gu = pl.pallas_call(
        kernel,
        out_shape=(
            jax.ShapeDtypeStruct((TOK, D), BF16),
            jax.ShapeDtypeStruct((RANK, 4096), F32),
            jax.ShapeDtypeStruct((RANK, D), F32),
        ),
        in_specs=[pl.BlockSpec(memory_space=pltpu.SMEM), hbm, hbm, hbm, hbm, vmem, hbm, vmem, hbm, hbm],
        out_specs=(vmem, vmem, vmem),
        scratch_shapes=[
            pltpu.VMEM((2, 3, SEQLEN, HEAD), BF16),
            pltpu.VMEM((SEQLEN, HEAD), F32),
            pltpu.VMEM((2, SEQLEN, HEAD), BF16),
            pltpu.VMEM((2, 4, CHIP, 1024), BF16),
            pltpu.VMEM((2, 1024, QUARTER), BF16),
            pltpu.VMEM((CHIP, HEAD), BF16),
            pltpu.VMEM((2, RANK, 1024), BF16),
            pltpu.VMEM((TOK, RANK), BF16),
            pltpu.VMEM((4, TOK, QUARTER), BF16),
            pltpu.VMEM((4, TOK, QUARTER), BF16),
            pltpu.VMEM((4, TOK, QUARTER), BF16),
            pltpu.VMEM((4, TOK, QUARTER), BF16),
            pltpu.VMEM((TOK, D), BF16),
            pltpu.VMEM((RANK, D), BF16),
            pltpu.VMEM((TOK, D), BF16),
            pltpu.VMEM((RANK, D), BF16),
            pltpu.VMEM((CHIP, HEAD), F32),
            pltpu.VMEM((TOK, HEAD), F32),
            pltpu.VMEM((32, D), BF16),
            pltpu.VMEM((32, D), BF16),
            pltpu.VMEM((8, 32, 640), BF16),
            pltpu.VMEM((2, RANK, 1024), BF16),
            pltpu.VMEM((8, 2, RANK, HEAD), BF16),
            pltpu.VMEM((8, 32, 640), BF16),
            pltpu.VMEM((8, RANK, 256), BF16),
            pltpu.VMEM((8, 32, 640), BF16),
            pltpu.VMEM((2, 8, RANK, 256), BF16),
            dma,
            dma((3,)),
            dma((2,)),
            dma,
            dma((2,)),
            dma((4,)),
            dma,
            dma((2, 2)),
            dma((2,)),
            dma,
            dma,
            dma,
            dma,
            dma,
            dma,
            dma,
            dma,
            dma((2,)),
            dma((2, 4)),
            dma((2, 4)),
        ],
        compiler_params=pltpu.CompilerParams(collective_id=1, has_side_effects=True, vmem_limit_bytes=63 * 2**20),
        cost_estimate=pl.CostEstimate(flops=18 * 10**9, bytes_accessed=30 * 10**6, transcendentals=19 * 10**6),
    )(lengths, q[0], k[0], v[0], res[0], gate, w, down.T, up, cot[0])
    return out[None], gd.T, gu


def solution(mesh):
    inner = Mesh(mesh.devices.reshape(4, 2, 4, 2, 2), AXES)
    return jax.shard_map(
        on_device,
        mesh=inner,
        in_specs=(
            P(DP, SEQ, None),
            P(DP, SEQ, None),
            P(DP, SEQ, None),
            P(DP, SEQ, None),
            P(DP, None),
            P(SEQ, None),
            P(),
            P(),
            P(DP, SEQ, None),
            P(DP),
        ),
        out_specs=(P(DP, SEQ, None), P(), P()),
        check_vma=False,
    )
```

time: 256 us -> 186 us (0.73); the launches traced: 253 us -> 186 us
  Pallas kernels: 243 us -> 178 us
  local copies, waits for them, and re-layouts: 8.73 us -> 5.79 us
    pallas_call x1, Pallas kernels: 243 us -> 178 us  [on_device(): pl.pallas_call(kernel, out_shape=(jax.ShapeDtypeStruct((TOK, D), BF16), j...]
    unnamed x8 -> x7, local copies, waits for them, and re-layouts: 8.73 us -> 5.79 us
where the time goes in v2:
time: 186 us
  Pallas kernels  178 us (96%)
  local copies, waits for them, and re-layouts  5.79 us (3%)
    pallas_call x1, Pallas kernels, on_device(): pl.pallas_call(kernel, out_shape=(jax.ShapeDtypeStruct((TOK, D), BF16), j...  178 us
    unnamed x7, local copies, waits for them, and re-layouts  5.79 us

profile of v2, /device:TPU:10, one launch (start us, length us, event | category | flops | bytes accessed | tf_op | source)
XLA Modules:
  0.0 185.5 jit_solution(5731741000660138921)
XLA Ops:
  1.3 178.4 %shard_map.121 = (bf16[192,5120]{1,0:T(8,128)(2,1)}, f32[64,4096]{1,0:T(8,128)}, f32[64,5120]{1,0:T(8,128)}) custom-call(s32[1]{0:T(128)S(6)} %copy.16.len_ref, bf16[192,4096]{1,0:T(8,128)(2,1)} %bitcast.12, bf16[192,4096]{1,0:T(8,128)(2,1)} %bitcast.13, bf16[192,4096]{1,0:T(8,128)(2,1)} %bitcast.14, bf16[192,5120]{1,0:T(8,128)(2,1)} %bitcast.10, ...), custom_call_target="tpu_custom_call" | custom-call | flops 17999998976 | bytes 30000000 | tf_op jit(solution)/shard_map/pallas_call | solution.py:400
  179.7 0.0 copy-start.1
  179.7 3.0 %copy.17 = bf16[1,192,5120]{2,1,0:T(8,128)(2,1)} copy(bf16[1,192,5120]{2,1,0:T(8,128)(2,1)} %bitcast.8) | data formatting | bytes 3932160
  182.8 0.0 copy-done.1
  182.8 0.0 copy-start
  182.8 1.0 copy.18
  183.7 0.7 copy-done
  184.5 1.1 copy.19
Async XLA Ops:
  179.7 3.0 %copy-start.1 = (f32[64,4096]{1,0:T(8,128)S(1)}, f32[64,4096]{1,0:T(8,128)}, u32[]{:S(2)}) copy-start(f32[64,4096]{1,0:T(8,128)} %get-tuple-element.7) | copy-start | bytes 3145732
  182.8 1.7 copy-start

commit v3 on v2

--- a/solution.py
+++ b/solution.py
@@ -52,6 +52,10 @@
 
     other = {"c": 1 - c}
 
+    def across(zz):
+        return {"z": zz, "yh": 1 - yh, "yl": 1 - yl}
+
+
     def remote(src, dst, sem, dev):
         return pltpu.make_async_remote_copy(
             src_ref=src, dst_ref=dst, send_sem=snd, recv_sem=sem, device_id=dev, device_id_type=MESH
@@ -67,7 +71,8 @@
             return 0
 
         lax.fori_loop(1, count + 1, step, 0)
-        pending.append((count, sample))
+        if sample is not None:
+            pending.append((count, sample))
 
     def landed(ref, sem):
         pltpu.make_async_copy(ref, ref, sem).wait()
@@ -94,13 +99,15 @@
 
     lax.fori_loop(1, 16, greet_seq, 0)
     lax.fori_loop(1, 8, greet_dp, 0)
+    for zz in range(4):
+        pl.semaphore_signal(barrier, inc=1, device_id=across(zz), device_id_type=MESH)
     loads = [
         pltpu.make_async_copy(src, dst, load_sem.at[n])
         for n, (src, dst) in enumerate(((cot_hbm, cot), (up_hbm, up), (res_hbm, res)))
     ]
     loads[0].start()
     loads[1].start()
-    pl.semaphore_wait(barrier, 22)
+    pl.semaphore_wait(barrier, 26)
 
     def send_head(h):
         def columns(p):
@@ -113,7 +120,8 @@
 
         for a, src in enumerate((q, k, v)):
             pltpu.make_async_copy(src.at[:, columns(s)], qkv.at[h, a, own], qkv_sem.at[h]).start()
-        send_all(15, start, qkv.at[0, 0, pl.ds(0, 3 * TOK)])
+        send_all(15, start, None)
+        pending.append((1, qkv.at[0, :, pl.ds(0, 15 * TOK)]))
 
     send_head(0)
     loads[2].start()
@@ -189,22 +197,31 @@
             return carry
 
         lax.fori_loop(0, SEQLEN // BQ, chunk, 0)
-        pending.append((7, att.at[0, pl.ds(0, CHIP), :]))
+        pending.append((1, att.at[0, pl.ds(0, 7 * CHIP), :]))
 
     def piece_columns(n):
         return pl.ds(pl.multiple_of(n * 256, 256), 256)
 
-    def send_weights(n, sem):
+    def send_weights(mine, theirs, sem):
+        place = pl.ds(pl.multiple_of(j * HEAD, HEAD), HEAD)
         for h in range(2):
-            cols = pl.ds(pl.multiple_of(x * QUARTER + n * 256, 256), 256)
-            src = w.at[pl.ds(h * HEAD, HEAD), cols]
-            dst = wq.at[h, pl.ds(pl.multiple_of(j * HEAD, HEAD), HEAD), piece_columns(n)]
-            pltpu.make_async_copy(src, dst, sem).start()
-            send_all(
-                7,
-                lambda d, src=src, dst=dst: remote(src, dst, sem, chip_peer(lax.rem(j + d, 8))).start(),
-                wq.at[0, pl.ds(0, HEAD), pl.ds(0, 256)],
-            )
+
+            def piece(n):
+                cols = pl.ds(pl.multiple_of(x * QUARTER + n * 256, 256), 256)
+                return w.at[pl.ds(h * HEAD, HEAD), cols], wq.at[h, place, piece_columns(n)]
+
+            near, far = piece(mine), piece(theirs)
+            pltpu.make_async_copy(*near, sem).start()
+
+            def start(d, near=near, far=far):
+                remote(*far, sem, across(lax.rem(z + d, 4))).start()
+
+                @pl.when(d < 4)
+                def _():
+                    remote(*near, sem, {"z": lax.rem(z + d, 4)}).start()
+
+            send_all(4, start, None)
+            pending.append((1, wq.at[0, pl.ds(0, 7 * HEAD), pl.ds(0, 256)]))
 
     def swap_weights():
         shared = wq.at[:, :, piece_columns(yl)]
@@ -225,12 +242,12 @@
     landed(qkv.at[0], qkv_sem.at[0])
     attend(0, {})
     landed(qkv.at[1], qkv_sem.at[1])
-    send_weights(yl, wq_sem.at[0])
-    attend(1, {1: lambda: forward(0), 2: swap_weights})
+    send_weights(yl, 1 - yl, wq_sem.at[0])
+    attend(1, {2: lambda: forward(0)})
     pending.append((2, ag.at[0, 0]))
     pending.append((1, wq.at[:, :, pl.ds(0, 256)]))
-    send_weights(2, wq_sem.at[1])
-    send_weights(3, wq_sem.at[2])
+    send_weights(2, 2, wq_sem.at[1])
+    swap_weights()
 
     forward_on(0)
     forward(1)
@@ -248,12 +265,12 @@
         cols = slice(t * 1024, (t + 1) * 1024)
         gup[:, cols] = lax.dot_general(low[...], scaled(cols), (((0,), (0,)), ((), ())), preferred_element_type=F32).astype(BF16)
     send(gup.at[pl.ds((1 - c) * 32, 32)], g0, g0_sem, other)
-    landed(g0, g0_sem)
-    gs[...] = (gup[pl.ds(c * 32, 32), :].astype(F32) + g0[...].astype(F32)).astype(BF16)
-
     landed(lgc.at[pl.ds(0, TOK)], lg_sem)
     for h in range(2):
         gdq[h] = lax.dot_general(lgc[...], ag[h, x], (((0,), (0,)), ((), ())), preferred_element_type=F32)[0:RANK].astype(BF16)
+
+    landed(g0, g0_sem)
+    gs[...] = (gup[pl.ds(c * 32, 32), :].astype(F32) + g0[...].astype(F32)).astype(BF16)
 
     def columns640(p):
         return pl.ds(pl.multiple_of(p * 640, 640), 640)
@@ -274,7 +291,8 @@
         lambda d: remote(gdq.at[:, :, head_columns(lax.rem(j + d, 8))], g1d.at[j], g1d_sem, chip_peer(lax.rem(j + d, 8))).start(),
         g1d.at[0],
     )
-    send_weights(4, wq_sem.at[3])
+    send_weights(3, 3, wq_sem.at[2])
+    send_weights(4, 4, wq_sem.at[3])
     forward_on(1)
 
     def total_of(ref):

time: 186 us -> 170 us (0.914)
  Pallas kernels: 178 us -> 162 us
    pallas_call x1, Pallas kernels: 178 us -> 162 us  [on_device(): pl.pallas_call(kernel, out_shape=(jax.ShapeDtypeStruct((TOK, D), BF16), j...]
where the time goes in v3:
time: 170 us; the launch traced here: 169 us
  Pallas kernels  162 us (95%)
  local copies, waits for them, and re-layouts  5.79 us (3%)
    pallas_call x1, Pallas kernels, on_device(): pl.pallas_call(kernel, out_shape=(jax.ShapeDtypeStruct((TOK, D), BF16), j...  162 us
    unnamed x7, local copies, waits for them, and re-layouts  5.79 us

profile of v3, /device:TPU:10, one launch (start us, length us, event | category | flops | bytes accessed | tf_op | source)
XLA Modules:
  0.0 169.3 jit_solution(15069330247820933246)
XLA Ops:
  1.3 162.3 %shard_map.121 = (bf16[192,5120]{1,0:T(8,128)(2,1)}, f32[64,4096]{1,0:T(8,128)}, f32[64,5120]{1,0:T(8,128)}) custom-call(s32[1]{0:T(128)S(6)} %copy.16.len_ref, bf16[192,4096]{1,0:T(8,128)(2,1)} %bitcast.12, bf16[192,4096]{1,0:T(8,128)(2,1)} %bitcast.13, bf16[192,4096]{1,0:T(8,128)(2,1)} %bitcast.14, bf16[192,5120]{1,0:T(8,128)(2,1)} %bitcast.10, ...), custom_call_target="tpu_custom_call" | custom-call | flops 17999998976 | bytes 30000000 | tf_op jit(solution)/shard_map/pallas_call | solution.py:418
  163.5 0.0 copy-start.1
  163.6 3.0 %copy.17 = bf16[1,192,5120]{2,1,0:T(8,128)(2,1)} copy(bf16[1,192,5120]{2,1,0:T(8,128)(2,1)} %bitcast.8) | data formatting | bytes 3932160
  166.6 0.0 copy-done.1
  166.6 0.0 copy-start
  166.6 1.0 copy.18
  167.6 0.7 copy-done
  168.3 1.1 copy.19
Async XLA Ops:
  163.5 3.0 %copy-start.1 = (f32[64,4096]{1,0:T(8,128)S(1)}, f32[64,4096]{1,0:T(8,128)}, u32[]{:S(2)}) copy-start(f32[64,4096]{1,0:T(8,128)} %get-tuple-element.7) | copy-start | bytes 3145732
  166.6 1.7 %copy-start = (f32[64,5120]{1,0:T(8,128)S(1)}, f32[64,5120]{1,0:T(8,128)}, u32[]{:S(2)}) copy-start(f32[64,5120]{1,0:T(8,128)} %get-tuple-element.14) | copy-start | bytes 3932164

commit v4 on v3

--- a/solution.py
+++ b/solution.py
@@ -109,19 +109,19 @@
     loads[1].start()
     pl.semaphore_wait(barrier, 26)
 
-    def send_head(h):
+    def send_head(h, which=(0, 1, 2)):
         def columns(p):
             return pl.ds(pl.multiple_of(p * 256 + h * HEAD, HEAD), HEAD)
 
         def start(d):
             p = lax.rem(s + d, 16)
-            for a, src in enumerate((q, k, v)):
+            for a, src in ((a, (q, k, v)[a]) for a in which):
                 remote(src.at[:, columns(p)], qkv.at[h, a, own], qkv_sem.at[h], seq_peer(p)).start()
 
-        for a, src in enumerate((q, k, v)):
+        for a, src in ((a, (q, k, v)[a]) for a in which):
             pltpu.make_async_copy(src.at[:, columns(s)], qkv.at[h, a, own], qkv_sem.at[h]).start()
         send_all(15, start, None)
-        pending.append((1, qkv.at[0, :, pl.ds(0, 15 * TOK)]))
+        pending.append((1, qkv.at[0, pl.ds(0, len(which)), pl.ds(0, 15 * TOK)]))
 
     send_head(0)
     loads[2].start()
@@ -147,7 +147,7 @@
             dn[h, :, t * HEAD : (t + 1) * HEAD] = down[:, pl.ds(pl.multiple_of(512 * t + 256 * c + 128 * h, HEAD), HEAD)]
 
     drain()
-    send_head(1)
+    send_head(1, (0, 1))
 
     def attend(h, between):
         def chunk(i, carry):
@@ -241,23 +241,34 @@
 
     landed(qkv.at[0], qkv_sem.at[0])
     attend(0, {})
+    send_head(1, (2,))
+    forward(0)
     landed(qkv.at[1], qkv_sem.at[1])
     send_weights(yl, 1 - yl, wq_sem.at[0])
-    attend(1, {2: lambda: forward(0)})
+    attend(1, {})
     pending.append((2, ag.at[0, 0]))
     pending.append((1, wq.at[:, :, pl.ds(0, 256)]))
     send_weights(2, 2, wq_sem.at[1])
     swap_weights()
 
     forward_on(0)
+
+    def grad_down_part(h):
+        gdq[h] = lax.dot_general(lgc[...], ag[h, x], (((0,), (0,)), ((), ())), preferred_element_type=F32)[0:RANK].astype(BF16)
+
+    def low_rank_part(h):
+        return lax.dot_general(ag[h, x], dn[h], (((1,), (1,)), ((), ())), preferred_element_type=F32)
+
+    landed(lgc.at[pl.ds(0, TOK)], lg_sem)
+    grad_down_part(0)
+    l0[...] = jnp.zeros((CHIP, HEAD), F32)
+    l0[:, 0:RANK] = low_rank_part(0)
     forward(1)
     pending.append((2, ag.at[0, 0]))
 
-    l0[...] = jnp.zeros((CHIP, HEAD), F32)
-    l0[:, 0:RANK] = lax.dot_general(
-        ag[0, x], dn[0], (((1,), (1,)), ((), ())), preferred_element_type=F32
-    ) + lax.dot_general(ag[1, x], dn[1], (((1,), (1,)), ((), ())), preferred_element_type=F32)
+    l0[:, 0:RANK] += low_rank_part(1)
     send(l0.at[pl.ds((1 - c) * TOK, TOK)], l1, lr_sem, other)
+    grad_down_part(1)
     landed(l1, lr_sem)
     low[...] = (l0[pl.ds(c * TOK, TOK), 0:RANK] + l1[:, 0:RANK]).astype(BF16)
 
@@ -265,10 +276,6 @@
         cols = slice(t * 1024, (t + 1) * 1024)
         gup[:, cols] = lax.dot_general(low[...], scaled(cols), (((0,), (0,)), ((), ())), preferred_element_type=F32).astype(BF16)
     send(gup.at[pl.ds((1 - c) * 32, 32)], g0, g0_sem, other)
-    landed(lgc.at[pl.ds(0, TOK)], lg_sem)
-    for h in range(2):
-        gdq[h] = lax.dot_general(lgc[...], ag[h, x], (((0,), (0,)), ((), ())), preferred_element_type=F32)[0:RANK].astype(BF16)
-
     landed(g0, g0_sem)
     gs[...] = (gup[pl.ds(c * 32, 32), :].astype(F32) + g0[...].astype(F32)).astype(BF16)
 
@@ -301,22 +308,23 @@
             total = total + ref[t].astype(F32)
         return total
 
-    landed(g1, g1_sem)
-    g2u[dp] = total_of(g1).astype(BF16)
-    landed(g1d, g1d_sem)
-    total = total_of(g1d)
-    for h in range(2):
-        g2d[dp, :, h * HEAD : (h + 1) * HEAD] = total[h].astype(BF16)
-    send_all(
-        7,
-        lambda d: remote(g2d.at[dp], g2d.at[dp], g2d_sem, dp_peer(lax.rem(dp + d, 8))).start(),
-        g2d.at[0],
-    )
-    send_all(
-        7,
-        lambda d: remote(g2u.at[dp], g2u.at[dp], g2u_sem, dp_peer(lax.rem(dp + d, 8))).start(),
-        g2u.at[0],
-    )
+    def over_clips():
+        landed(g1, g1_sem)
+        g2u[dp] = total_of(g1).astype(BF16)
+        landed(g1d, g1d_sem)
+        total = total_of(g1d)
+        for h in range(2):
+            g2d[dp, :, h * HEAD : (h + 1) * HEAD] = total[h].astype(BF16)
+        send_all(
+            7,
+            lambda d: remote(g2d.at[dp], g2d.at[dp], g2d_sem, dp_peer(lax.rem(dp + d, 8))).start(),
+            g2d.at[0],
+        )
+        send_all(
+            7,
+            lambda d: remote(g2u.at[dp], g2u.at[dp], g2u_sem, dp_peer(lax.rem(dp + d, 8))).start(),
+            g2u.at[0],
+        )
 
     groups = ((0, 3), (3, 2))
 
@@ -350,6 +358,8 @@
     def run_group(g):
         project(g, 1, right)
         project(g, 2, left)
+        if g == 0:
+            over_clips()
         finish(g, 1, right)
         if g == 0:
             for h in range(2):
@@ -368,16 +378,17 @@
     gda[c, j] = total_of(g2d).astype(BF16)
     landed(g2u.at[pl.ds(0, 7)], g2u_sem)
     g3u[j] = total_of(g2u).astype(BF16)
-    send_all(
-        7,
-        lambda d: remote(g3u.at[j], g3u.at[j], g3u_sem, chip_peer(lax.rem(j + d, 8))).start(),
-        g3u.at[0],
-    )
-    send_all(
-        7,
-        lambda d: remote(gda.at[c, j], gda.at[c, j], g3d_sem, chip_peer(lax.rem(j + d, 8))).start(),
-        gda.at[0, 0],
-    )
+    def spread(d):
+        for ref, sem in ((g3u.at[j], g3u_sem), (gda.at[c, j], g3d_sem)):
+            remote(ref, ref, sem, across(lax.rem(z + d, 4))).start()
+
+            @pl.when(d < 4)
+            def _():
+                remote(ref, ref, sem, {"z": lax.rem(z + d, 4)}).start()
+
+    send_all(4, spread, None)
+    pending.append((1, g3u.at[pl.ds(0, 7)]))
+    pending.append((1, gda.at[0, pl.ds(0, 7)]))
 
     landed(wq.at[:, :, pl.ds(0, 256)], wq_sem.at[2])
     landed(wq.at[:, :, pl.ds(0, 256)], wq_sem.at[3])
@@ -404,10 +415,10 @@
     landed(gda.at[0], g4_sem.at[1])
     rows_own, rows_other = (pl.ds(pl.multiple_of(r * 32, 32), 32) for r in (c, 1 - c))
     for t in range(8):
-        gu[rows_own, t * 640 : (t + 1) * 640] = g3u[t].astype(F32)
-        gu[rows_other, t * 640 : (t + 1) * 640] = g1[t].astype(F32)
+        gu[rows_own, t * 640 : (t + 1) * 640] = g3u[t]
+        gu[rows_other, t * 640 : (t + 1) * 640] = g1[t]
         for cc in range(2):
-            gd[:, (2 * t + cc) * 256 : (2 * t + cc + 1) * 256] = gda[cc, t].astype(F32)
+            gd[:, (2 * t + cc) * 256 : (2 * t + cc + 1) * 256] = gda[cc, t]
     drain()
 
 
@@ -419,8 +430,8 @@
         kernel,
         out_shape=(
             jax.ShapeDtypeStruct((TOK, D), BF16),
-            jax.ShapeDtypeStruct((RANK, 4096), F32),
-            jax.ShapeDtypeStruct((RANK, D), F32),
+            jax.ShapeDtypeStruct((RANK, 4096), BF16),
+            jax.ShapeDtypeStruct((RANK, D), BF16),
         ),
         in_specs=[pl.BlockSpec(memory_space=pltpu.SMEM), hbm, hbm, hbm, hbm, vmem, hbm, vmem, hbm, hbm],
         out_specs=(vmem, vmem, vmem),
@@ -476,7 +487,7 @@
         compiler_params=pltpu.CompilerParams(collective_id=1, has_side_effects=True, vmem_limit_bytes=63 * 2**20),
         cost_estimate=pl.CostEstimate(flops=18 * 10**9, bytes_accessed=30 * 10**6, transcendentals=19 * 10**6),
     )(lengths, q[0], k[0], v[0], res[0], gate, w, down.T, up, cot[0])
-    return out[None], gd.T, gu
+    return out[None], gd.T.astype(F32), gu.astype(F32)
 
 
 def solution(mesh):

time: 170 us -> 168 us (0.988)
  local copies, waits for them, and re-layouts: 5.79 us -> 1.28 us
  other arithmetic: 0 us -> 4.45 us
  Pallas kernels: 162 us -> 160 us
    unnamed x7 -> x3, local copies, waits for them, and re-layouts: 5.79 us -> 1.28 us
    convert_element_type x0 -> x2, other arithmetic: none -> 4.45 us  [on_device(): return (out[None], gd.T.astype(F32), gu.astype(F32))]
    pallas_call x1, Pallas kernels: 162 us -> 160 us  [on_device(): pl.pallas_call(kernel, out_shape=(jax.ShapeDtypeStruct((TOK, D), BF16), j...]
where the time goes in v4:
time: 168 us; the launch traced here: 167 us
  Pallas kernels  160 us (95%)
  other arithmetic  4.45 us (3%)
    pallas_call x1, Pallas kernels, on_device(): pl.pallas_call(kernel, out_shape=(jax.ShapeDtypeStruct((TOK, D), BF16), j...  160 us
    convert_element_type x2, other arithmetic, on_device(): return (out[None], gd.T.astype(F32), gu.astype(F32))  4.45 us

profile of v4, /device:TPU:10, one launch (start us, length us, event | category | flops | bytes accessed | tf_op | source)
XLA Modules:
  0.0 167.3 jit_solution(331646235718144970)
XLA Ops:
  1.3 160.3 %shard_map.121 = (bf16[192,5120]{1,0:T(8,128)(2,1)}, bf16[64,4096]{1,0:T(8,128)(2,1)}, bf16[64,5120]{1,0:T(8,128)(2,1)}) custom-call(s32[1]{0:T(128)S(6)} %copy.14.len_ref, bf16[192,4096]{1,0:T(8,128)(2,1)} %bitcast.12, bf16[192,4096]{1,0:T(8,128)(2,1)} %bitcast.13, bf16[192,4096]{1,0:T(8,128)(2,1)} %bitcast.14, bf16[192,5120]{1,0:T(8,128)(2,1)} %bitcast.10, ...), custom_call_target="tpu_custom_call" | custom-call | flops 17999998976 | bytes 30000000 | tf_op jit(solution)/shard_map/pallas_call | solution.py:429
  161.6 0.0 copy-start
  161.6 2.2 %convert_bitcast_fusion = f32[4096,64]{0,1:T(8,128)} fusion(bf16[64,4096]{1,0:T(8,128)(2,1)} %get-tuple-element.7), kind=kLoop, calls=%fused_computation | loop fusion | flops 262144 | bytes 1572864 | tf_op jit(solution)/shard_map/convert_element_type | solution.py:490
  163.8 2.2 %convert_element_type.11 = f32[64,5120]{1,0:T(8,128)} convert(bf16[64,5120]{1,0:T(8,128)(2,1)} %get-tuple-element.8) | non-fusion elementwise | flops 327680 | bytes 1966080 | tf_op jit(solution)/shard_map/convert_element_type | solution.py:490
  166.1 0.0 copy-done
  166.1 1.3 copy.15
Async XLA Ops:
  161.6 4.5 %copy-start = (bf16[192,5120]{1,0:T(8,128)(2,1)S(1)}, bf16[192,5120]{1,0:T(8,128)(2,1)}, u32[]{:S(2)}) copy-start(bf16[192,5120]{1,0:T(8,128)(2,1)} %get-tuple-element.6) | copy-start | bytes 5898244
